TPU v7x, 32 devices: a whole 2x2x4 slice. The times are simulated.
32 devices in a mesh: ctx: 4 (over z), head: 4 (over x, core), side: 2 (over y).
Axes of the slice: x: 2, y: 2, z: 4, core: 2. Of those that a mesh axis runs over, the one named last changes fastest.
Arguments:
- prefill_query: bfloat16 [1024, 64, 128], P('ctx', ('head', 'side')), may hold values from -6 to 6
- prefill_keys: bfloat16 [1024, 8, 128], P('ctx', ('head', 'side')), may hold values from -6 to 6
- prefill_values: bfloat16 [1024, 8, 128], P('ctx', ('head', 'side')), may hold values from -6 to 6
- token_pos: int32 [1024], P('ctx'), may hold values from 0 to 1023, as said below
- scale_exp: int32 [16, 8, 2], P('ctx', ('head', 'side')), may hold values from -7 to -5
- page_owner: int32 [16], P('ctx'), may hold values from 0 to 3, as said below
- draft_query: bfloat16 [256, 64, 128], P(None, ('head', 'side')), may hold values from -6 to 6
- draft_keys: bfloat16 [256, 8, 128], P('side', 'head'), may hold values from -6 to 6
- draft_values: bfloat16 [256, 8, 128], P('side', 'head'), may hold values from -6 to 6
- parents: int32 [256], replicated, may hold values from 0 to 254, as said below
Outputs:
- prefill_out: bfloat16 [1024, 64, 128], P('ctx', ('head', 'side'))
- cache_keys: bfloat16 [1024, 8, 128], P('ctx', ('head', 'side'))
- cache_values: bfloat16 [1024, 8, 128], P('ctx', ('head', 'side'))
- verify_out: bfloat16 [256, 64, 128], P('ctx', ('head', 'side'))
Inputs may be any that keep to these rules, and one draw needn't show every extreme that they name: `token_pos`: a permutation of 0 to 1023; the rows of shard c of ctx hold the runs a and 2 * 4 - 1 - a of 128 consecutive positions, in order, with a different a for each shard. `page_owner`: the 16 // 4 entries of one ctx shard are a permutation of 0 to 4 - 1. parents[0] = 0, and parents[r] < r for r >= 1.
All inputs are finite; a program needn't handle non-finite values.
Results may differ from a plain program's by a relative error of at most 0.0049.
Values may be sent and summed in bfloat16 or wider, within the bound.
A program may use at most 64 MiB of HBM per device.

v0:
```python
import math

import jax
import jax.numpy as jnp
import numpy as np
from jax import lax
from jax.sharding import PartitionSpec as P

NEG_FILL = -1e30
FP_LIMIT = 448.0
LOG_TWO_E = 1.4426950408889634


def power_two(exponent):
    levels = jnp.arange(-7, -4, dtype=jnp.int32)
    table = jnp.asarray(np.array([2.0**level for level in range(-7, -4)], np.float32))
    return jnp.sum(jnp.where(exponent[..., None] == levels, table, jnp.float32(0.0)), axis=-1)


def ancestors(parent_rows):
    row_total = parent_rows.shape[0]
    row_index = jnp.arange(row_total, dtype=jnp.int32)
    linked = (
        (parent_rows[:, None] == row_index[None, :]) | (row_index[:, None] == row_index[None, :])
    ).astype(jnp.float32)
    for _ in range(row_total.bit_length()):
        linked = jnp.minimum(
            jnp.dot(linked, linked, precision=lax.Precision.HIGHEST), jnp.float32(1.0)
        )
    return linked > 0.5


def online_step(running, scores, allowed, value_block):
    old_top, old_mass, old_numer = running
    block_top = jnp.ceil(LOG_TWO_E * jnp.max(jnp.where(allowed, scores, NEG_FILL), axis=1))
    new_top = jnp.maximum(old_top, block_top)
    weights = jnp.where(allowed, jnp.exp2(LOG_TWO_E * scores - new_top[:, None]), jnp.float32(0.0))
    factor = jnp.exp2(old_top - new_top)
    new_mass = old_mass * factor + jnp.sum(weights, axis=1)
    new_numer = old_numer * factor[:, None] + jnp.dot(
        weights.astype(jnp.bfloat16), value_block, preferred_element_type=jnp.float32
    )
    return (new_top, new_mass, new_numer)


def body(
    prefill_query,
    prefill_keys,
    prefill_values,
    token_pos,
    scale_exp,
    page_owner,
    draft_query,
    draft_keys,
    draft_values,
    parents,
):
    tok_rows, groups, width = prefill_query.shape
    scale_factor = width ** (-0.5)
    shard_total = lax.axis_size("ctx")
    page_rows = tok_rows // shard_total
    my_index = lax.axis_index("ctx")
    query_rows = prefill_query.reshape(tok_rows * groups, width)
    query_places = jnp.repeat(token_pos, groups)
    local_keys = prefill_keys.reshape(tok_rows, width)
    local_values = prefill_values.reshape(tok_rows, width)
    page_scales = power_two(scale_exp.reshape(shard_total, 2))
    start_state = (
        jnp.full((tok_rows * groups,), NEG_FILL, jnp.float32),
        jnp.zeros((tok_rows * groups,), jnp.float32),
        jnp.zeros((tok_rows * groups, width), jnp.float32),
    )

    def attend(running, key_block, value_block, place_block):
        scores = scale_factor * jnp.einsum(
            "qd,kd->qk", query_rows, key_block, preferred_element_type=jnp.float32
        )
        allowed = query_places[:, None] >= place_block[None, :]
        return online_step(running, scores, allowed, value_block)

    running = start_state
    key_piece = lax.all_gather(local_keys, "ctx", axis=0, tiled=True)
    value_piece = lax.all_gather(local_values, "ctx", axis=0, tiled=True)
    place_piece = lax.all_gather(token_pos, "ctx", axis=0, tiled=True)
    row_count = key_piece.shape[0]
    block_rows = math.gcd(row_count, 512)
    block_total = row_count // block_rows

    def inner_rows(carry_in, item):
        return (attend(carry_in, item[0], item[1], item[2]), None)

    running, _ = lax.scan(
        inner_rows,
        running,
        (
            key_piece.reshape(block_total, block_rows, width),
            value_piece.reshape(block_total, block_rows, width),
            place_piece.reshape(block_total, block_rows),
        ),
    )
    paged_keys = local_keys.reshape(shard_total, page_rows, width).astype(jnp.float32)
    paged_values = local_values.reshape(shard_total, page_rows, width).astype(jnp.float32)
    scaled_keys = jnp.clip(paged_keys / page_scales[:, 0, None, None], -FP_LIMIT, FP_LIMIT).astype(
        jnp.bfloat16
    )
    scaled_values = jnp.clip(
        paged_values / page_scales[:, 1, None, None], -FP_LIMIT, FP_LIMIT
    ).astype(jnp.bfloat16)
    slot_index = jnp.arange(shard_total, dtype=jnp.int32)
    inverse = jnp.sum(
        jnp.where(page_owner[None, :] == slot_index[:, None], slot_index[None, :], 0), axis=1
    )
    got_keys, got_values, got_scales = (
        lax.all_to_all(
            jnp.take(scaled_keys, inverse, axis=0), "ctx", split_axis=0, concat_axis=0, tiled=True
        ),
        lax.all_to_all(
            jnp.take(scaled_values, inverse, axis=0), "ctx", split_axis=0, concat_axis=0, tiled=True
        ),
        lax.all_to_all(
            jnp.take(page_scales, inverse, axis=0).astype(jnp.bfloat16),
            "ctx",
            split_axis=0,
            concat_axis=0,
            tiled=True,
        ),
    )
    scale_back = got_scales.astype(jnp.float32)
    cache_keys = (
        (got_keys.astype(jnp.float32) * scale_back[:, 0, None, None])
        .astype(jnp.bfloat16)
        .reshape(tok_rows, width)
    )
    cache_values = (
        (got_values.astype(jnp.float32) * scale_back[:, 1, None, None])
        .astype(jnp.bfloat16)
        .reshape(tok_rows, width)
    )
    prefill_out = (
        (running[2] / running[1][:, None]).astype(jnp.bfloat16).reshape(tok_rows, groups, width)
    )
    tree_keys, tree_values = (
        lax.all_to_all(draft_keys, "side", split_axis=1, concat_axis=0, tiled=True),
        lax.all_to_all(draft_values, "side", split_axis=1, concat_axis=0, tiled=True),
    )
    row_total = draft_query.shape[0]
    tree_keys = tree_keys.reshape(row_total, width)
    tree_values = tree_values.reshape(row_total, width)
    draft_rows = draft_query.reshape(row_total * groups, width)
    cache_scores = scale_factor * jnp.einsum(
        "qd,kd->qk", draft_rows, cache_keys, preferred_element_type=jnp.float32
    )
    cache_top = jnp.ceil(LOG_TWO_E * jnp.max(cache_scores, axis=1))
    tree_mask = jnp.repeat(ancestors(parents), groups, axis=0)
    tree_scores = scale_factor * jnp.einsum(
        "qd,kd->qk", draft_rows, tree_keys, preferred_element_type=jnp.float32
    )
    tree_top = jnp.ceil(LOG_TWO_E * jnp.max(jnp.where(tree_mask, tree_scores, NEG_FILL), axis=1))
    tree_weights = jnp.where(
        tree_mask, jnp.exp2(LOG_TWO_E * tree_scores - tree_top[:, None]), jnp.float32(0.0)
    )
    tree_mass = jnp.sum(tree_weights, axis=1)
    tree_numer = jnp.dot(
        tree_weights.astype(jnp.bfloat16), tree_values, preferred_element_type=jnp.float32
    )
    share_rows = row_total // shard_total

    def own_rows(array):
        return lax.dynamic_slice_in_dim(array, my_index * share_rows, share_rows, 0)

    global_top = lax.pmax(cache_top, "ctx")
    cache_weights = jnp.exp2(LOG_TWO_E * cache_scores - global_top[:, None])
    cache_mass = jnp.sum(cache_weights, axis=1).reshape(row_total, groups)
    cache_numer = jnp.dot(
        cache_weights.astype(jnp.bfloat16), cache_values, preferred_element_type=jnp.float32
    ).reshape(row_total, groups, width)
    far_mass, far_numer = (
        lax.psum_scatter(cache_mass, "ctx", scatter_dimension=0, tiled=True),
        lax.psum_scatter(cache_numer, "ctx", scatter_dimension=0, tiled=True),
    )
    far_top = own_rows(global_top.reshape(row_total, groups))
    near_top = own_rows(tree_top.reshape(row_total, groups))
    near_mass = own_rows(tree_mass.reshape(row_total, groups))
    near_numer = own_rows(tree_numer.reshape(row_total, groups, width))
    joint_top = jnp.maximum(far_top, near_top)
    far_factor = jnp.exp2(far_top - joint_top)
    near_factor = jnp.exp2(near_top - joint_top)
    numer_total = far_numer * far_factor[..., None] + near_numer * near_factor[..., None]
    mass_total = far_mass * far_factor + near_mass * near_factor
    verify_out = (numer_total / mass_total[..., None]).astype(jnp.bfloat16)
    return (
        prefill_out,
        cache_keys.reshape(tok_rows, 1, width),
        cache_values.reshape(tok_rows, 1, width),
        verify_out,
    )


def solution(mesh):
    return jax.shard_map(
        body,
        mesh=mesh,
        in_specs=(
            P("ctx", ("head", "side"), None),
            P("ctx", ("head", "side"), None),
            P("ctx", ("head", "side"), None),
            P("ctx"),
            P("ctx", ("head", "side"), None),
            P("ctx"),
            P(None, ("head", "side"), None),
            P("side", "head", None),
            P("side", "head", None),
            P(),
        ),
        out_specs=(
            P("ctx", ("head", "side"), None),
            P("ctx", ("head", "side"), None),
            P("ctx", ("head", "side"), None),
            P("ctx", ("head", "side"), None),
        ),
        check_vma=False,
    )
```

profile of v0, /device:TPU:0, one launch (start us, length us, event | category | flops | bytes accessed | tf_op | source)
XLA Modules:
  0.0 165.0 jit_solution(2705002931016988537)
XLA Ops:
  7.2 0.8 select_reduce_fusion
  8.0 0.8 fusion.50
  8.8 0.1 copy.72
  8.9 0.6 gather_fusion
  9.5 0.1 copy.73
  9.6 0.7 copy.74
  10.3 6.3 %all-to-all-start.1 = ((bf16[4,1,2]{2,1,0:T(2,128)(2,1)}), bf16[4,1,2]{2,1,0:T(2,128)(2,1)S(1)}, u32[]{:S(2)}, u32[]{:S(2)}) async-start(bf16[4,1,2]{2,1,0:T(2,128)(2,1)} %copy.74), calls=%async_computation.1 | async-start | bytes 4096 | tf_op jit(solution)/shard_map/all_to_all | solution.py:120
  16.6 11.6 %all-gather.2 = s32[4,1,256]{2,1,0:T(1,128)S(1)} all-gather(s32[1,1,256]{2,1,0:T(1,128)} %bitcast.141), channel_id=1, replica_groups=mesh['ctx'=4,'head'=4,'side'=2] {'ctx'}, dimensions={0}, use_global_device_ids=true | all-gather | bytes 5120 | tf_op jit(solution)/shard_map/all_gather | solution.py:84
  28.3 14.1 %all-gather = bf16[1024,1,128]{2,0,1:T(8,128)(2,1)S(1)} all-gather(bf16[256,1,128]{2,0,1:T(8,128)(2,1)} %param.16), channel_id=2, replica_groups=mesh['ctx'=4,'head'=4,'side'=2] {'ctx'}, dimensions={0}, use_global_device_ids=true | all-gather | bytes 327680 | tf_op jit(solution)/shard_map/all_gather | solution.py:82
  42.4 14.4 %all-gather.1 = bf16[1024,1,128]{2,0,1:T(8,128)(2,1)S(1)} all-gather(bf16[256,1,128]{2,0,1:T(8,128)(2,1)} %param.17), channel_id=3, replica_groups=mesh['ctx'=4,'head'=4,'side'=2] {'ctx'}, dimensions={0}, use_global_device_ids=true | all-gather | bytes 327680 | tf_op jit(solution)/shard_map/all_gather | solution.py:83
  56.8 19.7 %while.17 = (s32[]{:T(128)}, f32[2048]{0:T(1024)S(1)}, f32[2048]{0:T(1024)S(1)}, f32[2048,128]{1,0:T(8,128)S(1)}, s32[2,512]{1,0:T(2,128)S(1)}, /*index=5*/bf16[...) while((s32[]{:T(128)}, f32[2048]{0:T(1024)S(1)}, ...), condition=%wide.region_3.4_spmd.clone, body=%wide.region_0.3_spmd.clone.sunk | while | flops 554450944 | bytes 32435368 | solution.py:92
  56.8 0.8 broadcast_in_dim.140
  57.6 0.1 ge.93
  57.8 3.7 %fusion.85 = (f32[2048]{0:T(1024)S(1)}, f32[512,2048]{1,0:T(8,128)}) fusion(s32[2048]{0:T(1024)S(1)} %ge.93, s32[512]{0:T(512)S(1)} %bitcast.138, bf16[2048,128]{1,0:T(8,128)(2,1)} %get-tuple-element.310, bf16[2,512,128]{2,1,0:T(8,128)(2,1)S(1)} %get-tuple-element.309, s32[]{:T(128)S(6)} %copy.99), kind=kOutput, calls=%fused_computation.6.clone.1 | convolution fusion | flops 272627712 | bytes 4868100 | tf_op jit(solution)/shard_map/while/body/eval_jaxpr/qd,kd->qk/dot_general | solution.py:75
  61.5 3.5 %fusion.86 = f32[2048]{0:T(1024)S(1)} fusion(f32[512,2048]{1,0:T(8,128)} %get-tuple-element.279, f32[2048]{0:T(1024)S(1)} %ceil_maximum_fusion.2, s32[2048]{0:T(1024)S(1)} %ge.93, s32[512]{0:T(512)S(1)} %bitcast.139), kind=kLoop, calls=%fused_computation.8.clone.1 | loop fusion | flops 6289408 | bytes 4220928 | tf_op jit(solution)/shard_map/while/body/eval_jaxpr/reduce_sum | solution.py:39
  65.0 1.7 %convolution_add_fusion.2 = f32[2048,128]{1,0:T(8,128)S(1)} fusion(f32[512,2048]{1,0:T(8,128)S(1)} %copy-done.1, f32[2048]{0:T(1024)S(1)} %ceil_maximum_fusion.2, s32[2048]{0:T(1024)S(1)} %ge.93, s32[512]{0:T(512)S(1)} %bitcast.140, f32[2048,128]{1,0:T(8,128)S(1)} %get-tuple-element.296, f32[2048]{0:T(1024)S(1)} %get-tuple-element.281, ...), kind=kOutput, calls=%fused_computation.9.clone.1 | convolution fusion | flops 275513344 | bytes 6449157 | tf_op jit(solution)/shard_map/while/body/eval_jaxpr/dot_general | solution.py:40
  66.7 0.8 broadcast_in_dim.140
  67.5 0.1 ge.93
  67.6 3.7 %fusion.85 = (f32[2048]{0:T(1024)S(1)}, f32[512,2048]{1,0:T(8,128)}) fusion(s32[2048]{0:T(1024)S(1)} %ge.93, s32[512]{0:T(512)S(1)} %bitcast.138, bf16[2048,128]{1,0:T(8,128)(2,1)} %get-tuple-element.310, bf16[2,512,128]{2,1,0:T(8,128)(2,1)S(1)} %get-tuple-element.309, s32[]{:T(128)S(6)} %copy.99), kind=kOutput, calls=%fused_computation.6.clone.1 | convolution fusion | flops 272627712 | bytes 4868100 | tf_op jit(solution)/shard_map/while/body/eval_jaxpr/qd,kd->qk/dot_general | solution.py:75
  71.4 3.5 %fusion.86 = f32[2048]{0:T(1024)S(1)} fusion(f32[512,2048]{1,0:T(8,128)} %get-tuple-element.279, f32[2048]{0:T(1024)S(1)} %ceil_maximum_fusion.2, s32[2048]{0:T(1024)S(1)} %ge.93, s32[512]{0:T(512)S(1)} %bitcast.139), kind=kLoop, calls=%fused_computation.8.clone.1 | loop fusion | flops 6289408 | bytes 4220928 | tf_op jit(solution)/shard_map/while/body/eval_jaxpr/reduce_sum | solution.py:39
  74.9 1.7 %convolution_add_fusion.2 = f32[2048,128]{1,0:T(8,128)S(1)} fusion(f32[512,2048]{1,0:T(8,128)S(1)} %copy-done.1, f32[2048]{0:T(1024)S(1)} %ceil_maximum_fusion.2, s32[2048]{0:T(1024)S(1)} %ge.93, s32[512]{0:T(512)S(1)} %bitcast.140, f32[2048,128]{1,0:T(8,128)S(1)} %get-tuple-element.296, f32[2048]{0:T(1024)S(1)} %get-tuple-element.281, ...), kind=kOutput, calls=%fused_computation.9.clone.1 | convolution fusion | flops 275513344 | bytes 6449157 | tf_op jit(solution)/shard_map/while/body/eval_jaxpr/dot_general | solution.py:40
  76.6 0.1 fusion.42
  76.7 0.6 gather_fusion.2
  77.3 0.1 fusion.44
  77.4 0.6 gather_fusion.1
  77.9 0.3 convolution_minimum_fusion.8
  78.2 0.4 convolution_minimum_fusion.7
  78.6 0.4 convolution_minimum_fusion.6
  79.0 0.4 convolution_minimum_fusion.5
  79.4 0.4 convolution_minimum_fusion.4
  79.8 0.4 convolution_minimum_fusion.3
  80.2 0.4 convolution_minimum_fusion.2
  80.6 0.6 copy.79
  81.2 0.7 broadcast_select_fusion
  81.9 3.3 %all-to-all-start = ((bf16[4,64,128]{2,1,0:T(8,128)(2,1)}), bf16[4,64,128]{2,1,0:T(8,128)(2,1)S(1)}, u32[]{:S(2)}, u32[]{:S(2)}) async-start(bf16[4,64,128]{2,1,0:T(8,128)(2,1)} %get-tuple-element.212), calls=%async_computation | async-start | bytes 131072 | tf_op jit(solution)/shard_map/all_to_all | solution.py:114
  85.2 0.1 copy.75
  85.3 5.6 %all-to-all-done = bf16[4,64,128]{2,1,0:T(8,128)(2,1)S(1)} async-done(((bf16[4,64,128]{2,1,0:T(8,128)(2,1)}), bf16[4,64,128]{2,1,0:T(8,128)(2,1)S(1)}, u32[]{:S(2)}, u32[]{:S(2)}) %all-to-all-start) | async-done | bytes 65568 | tf_op jit(solution)/shard_map/all_to_all | solution.py:114
  90.9 3.3 %all-to-all-start.2 = ((bf16[4,64,128]{2,1,0:T(8,128)(2,1)}), bf16[4,64,128]{2,1,0:T(8,128)(2,1)S(1)}, u32[]{:S(2)}, u32[]{:S(2)}) async-start(bf16[4,64,128]{2,1,0:T(8,128)(2,1)} %get-tuple-element.211), calls=%async_computation.2 | async-start | bytes 131072 | tf_op jit(solution)/shard_map/all_to_all | solution.py:117
  94.3 0.1 multiply_convert_fusion.1
  94.4 0.4 multiply_reduce_fusion
  94.9 12.3 %pmax.7 = f32[2048]{0:T(1024)S(1)} all-reduce(f32[2048]{0:T(1024)S(1)} %multiply_ceil_fusion.1), channel_id=1, replica_groups=mesh['ctx'=4,'head'=4,'side'=2] {'ctx'}, use_global_device_ids=true, to_apply=%region_7.9 | all-reduce | flops 2048 | bytes 16384 | tf_op jit(solution)/shard_map/pmax | solution.py:171
  107.1 1.4 fusion.23
  108.5 1.6 copy.76
  110.1 0.8 reshape.205
  110.9 3.3 %all-to-all-start.3 = ((bf16[128,2,128]{2,0,1:T(8,128)(2,1)}), bf16[128,2,128]{2,0,1:T(8,128)(2,1)S(1)}, u32[]{:S(2)}, u32[]{:S(2)}) async-start(bf16[128,2,128]{2,0,1:T(8,128)(2,1)} %copy.79), calls=%async_computation.4 | async-start | bytes 131072 | tf_op jit(solution)/shard_map/all_to_all | solution.py:143
  114.3 0.1 multiply_convert_fusion
  114.4 1.5 fusion.32
  115.9 0.4 convolution_minimum_fusion.1
  116.3 1.1 fusion.38
  117.4 0.4 fusion.27
  117.8 0.6 copy.81
  118.4 3.5 %all-to-all-start.4 = ((bf16[128,2,128]{2,0,1:T(8,128)(2,1)}), bf16[128,2,128]{2,0,1:T(8,128)(2,1)S(1)}, u32[]{:S(2)}, u32[]{:S(2)}) async-start(bf16[128,2,128]{2,0,1:T(8,128)(2,1)} %copy.81), calls=%async_computation.5 | async-start | bytes 131072 | tf_op jit(solution)/shard_map/all_to_all | solution.py:144
  121.9 0.7 fusion.22
  122.6 0.1 ceil.22
  122.7 1.8 %fusion.25 = (f32[2048]{0:T(1024)S(1)}, bf16[256,8,256]{2,1,0:T(8,128)(2,1)}) fusion(f32[2048,256]{1,0:T(8,128)S(1)} %get-tuple-element.214, f32[2048]{0:T(1024)S(1)} %multiply_ceil_fusion, pred[256,256]{1,0:T(8,128)(4,1)S(1)} %fusion.27), kind=kLoop, calls=%fused_computation.38 | loop fusion | flops 3143680 | bytes 3227648 | tf_op jit(solution)/shard_map/reduce_sum | solution.py:162
  124.5 0.1 reshape.162
  124.8 1.2 all-to-all-done.4
  126.0 1.7 %fusion.30 = f32[256,8,128]{2,0,1:T(8,128)S(1)} fusion(bf16[256,128,1]{1,0,2:T(8,128)(2,1)S(1)} %bitcast.135, bf16[256,8,256]{2,1,0:T(8,128)(2,1)} %get-tuple-element.204), kind=kOutput, calls=%fused_computation.52 | convolution fusion | flops 134217728 | bytes 2162688 | tf_op jit(solution)/shard_map/dot_general | solution.py:163
  127.7 0.1 reshape.157
  127.9 0.6 reduce-scatter.7.cloned.1.call-done
  128.5 0.8 copy.87
  129.3 26.9 %reduce-scatter.5.cloned.1.call-done = f32[64,8,128]{2,0,1:T(8,128)} async-done(((f32[256,8,128]{2,0,1:T(8,128)}), f32[64,8,128]{2,0,1:T(8,128)}) %reduce-scatter.5.cloned.1.call-update) | async-done | bytes 262160 | tf_op jit(solution)/shard_map/reduce_scatter | solution.py:179
  156.1 1.2 divide_convert_fusion.1
  157.4 0.7 copy.85
  (62 shorter events, 0.6 us)
Async XLA Ops:
  7.2 87.2 %copy-start = (bf16[256,8,128]{2,1,0:T(8,128)(2,1)S(1)}, bf16[256,8,128]{2,1,0:T(8,128)(2,1)}, u32[]{:S(2)}) copy-start(bf16[256,8,128]{2,1,0:T(8,128)(2,1)} %param.21) | copy-start | bytes 1572868
  10.3 71.6 %all-to-all-start.1 = ((bf16[4,1,2]{2,1,0:T(2,128)(2,1)}), bf16[4,1,2]{2,1,0:T(2,128)(2,1)S(1)}, u32[]{:S(2)}, u32[]{:S(2)}) async-start(bf16[4,1,2]{2,1,0:T(2,128)(2,1)} %copy.74), calls=%async_computation.1 | async-start | bytes 4096 | tf_op jit(solution)/shard_map/all_to_all | solution.py:120
  56.8 19.8 %copy-start.4 = (bf16[256,1,128]{2,0,1:T(8,128)(2,1)S(1)}, bf16[256,1,128]{2,0,1:T(8,128)(2,1)}, u32[]{:S(2)}) copy-start(bf16[256,1,128]{2,0,1:T(8,128)(2,1)} %param.17) | copy-start | bytes 196612
  56.8 20.4 %copy-start.5 = (bf16[256,1,128]{2,0,1:T(8,128)(2,1)S(1)}, bf16[256,1,128]{2,0,1:T(8,128)(2,1)}, u32[]{:S(2)}) copy-start(bf16[256,1,128]{2,0,1:T(8,128)(2,1)} %param.16) | copy-start | bytes 196612
  56.8 21.1 %copy-start.10 = (s32[256]{0:T(256)S(1)}, s32[256]{0:T(256)}, u32[]{:S(2)}) copy-start(s32[256]{0:T(256)} %param.24) | copy-start | bytes 3076
  61.5 3.5 %copy-start.1 = (f32[512,2048]{1,0:T(8,128)S(1)}, f32[512,2048]{1,0:T(8,128)}, u32[]{:S(2)}) copy-start(f32[512,2048]{1,0:T(8,128)} %get-tuple-element.279) | copy-start | bytes 12582916 | tf_op jit(solution)/shard_map/while
  71.3 3.5 %copy-start.1 = (f32[512,2048]{1,0:T(8,128)S(1)}, f32[512,2048]{1,0:T(8,128)}, u32[]{:S(2)}) copy-start(f32[512,2048]{1,0:T(8,128)} %get-tuple-element.279) | copy-start | bytes 12582916 | tf_op jit(solution)/shard_map/while
  76.6 17.8 %copy-start.2 = (f32[2048,128]{1,0:T(8,128)}, f32[2048,128]{1,0:T(8,128)S(1)}, u32[]{:S(2)}) copy-start(f32[2048,128]{1,0:T(8,128)S(1)} %get-tuple-element.119) | copy-start | bytes 3145732
  76.6 4.0 %copy-start.8 = (bf16[128,2,128]{2,1,0:T(2,128)(2,1)S(1)}, bf16[128,2,128]{2,1,0:T(2,128)(2,1)}, u32[]{:S(2)}) copy-start(bf16[128,2,128]{2,1,0:T(2,128)(2,1)} %param.22) | copy-start | bytes 196612
  81.9 9.0 %all-to-all-start = ((bf16[4,64,128]{2,1,0:T(8,128)(2,1)}), bf16[4,64,128]{2,1,0:T(8,128)(2,1)S(1)}, u32[]{:S(2)}, u32[]{:S(2)}) async-start(bf16[4,64,128]{2,1,0:T(8,128)(2,1)} %get-tuple-element.212), calls=%async_computation | async-start | bytes 131072 | tf_op jit(solution)/shard_map/all_to_all | solution.py:114
  90.9 20.0 %all-to-all-start.2 = ((bf16[4,64,128]{2,1,0:T(8,128)(2,1)}), bf16[4,64,128]{2,1,0:T(8,128)(2,1)S(1)}, u32[]{:S(2)}, u32[]{:S(2)}) async-start(bf16[4,64,128]{2,1,0:T(8,128)(2,1)} %get-tuple-element.211), calls=%async_computation.2 | async-start | bytes 131072 | tf_op jit(solution)/shard_map/all_to_all | solution.py:117
  94.2 34.2 %reduce-scatter.7.cloned.1.call-start = ((), (), s32[]{:S(2)}) async-start(), calls=%async_computation.8 | async-start | bytes 163840
  94.4 16.5 %copy-start.7 = (bf16[4,64,128]{2,1,0:T(8,128)(2,1)}, bf16[4,64,128]{2,1,0:T(8,128)(2,1)S(1)}, u32[]{:S(2)}) copy-start(bf16[4,64,128]{2,1,0:T(8,128)(2,1)S(1)} %multiply_convert_fusion.1) | copy-start | bytes 196612
  108.5 7.7 %copy-start.3 = (f32[2048,128]{1,0:T(8,128)S(1)}, f32[2048,128]{1,0:T(8,128)}, u32[]{:S(2)}) copy-start(f32[2048,128]{1,0:T(8,128)} %copy-done.2) | copy-start | bytes 3145732
  108.5 9.2 %copy-start.9 = (bf16[128,2,128]{2,1,0:T(2,128)(2,1)S(1)}, bf16[128,2,128]{2,1,0:T(2,128)(2,1)}, u32[]{:S(2)}) copy-start(bf16[128,2,128]{2,1,0:T(2,128)(2,1)} %param.23) | copy-start | bytes 196612
  110.9 7.5 %all-to-all-start.3 = ((bf16[128,2,128]{2,0,1:T(8,128)(2,1)}), bf16[128,2,128]{2,0,1:T(8,128)(2,1)S(1)}, u32[]{:S(2)}, u32[]{:S(2)}) async-start(bf16[128,2,128]{2,0,1:T(8,128)(2,1)} %copy.79), calls=%async_computation.4 | async-start | bytes 131072 | tf_op jit(solution)/shard_map/all_to_all | solution.py:143
  114.2 41.9 %reduce-scatter.5.cloned.1.call-start = ((), (), s32[]{:S(2)}) async-start(), calls=%async_computation.7 | async-start | bytes 1310720 | tf_op jit(solution)/shard_map/reduce_scatter | solution.py:179
  114.4 8.2 %copy-start.6 = (bf16[4,64,128]{2,1,0:T(8,128)(2,1)}, bf16[4,64,128]{2,1,0:T(8,128)(2,1)S(1)}, u32[]{:S(2)}) copy-start(bf16[4,64,128]{2,1,0:T(8,128)(2,1)S(1)} %multiply_convert_fusion) | copy-start | bytes 196612
  118.4 7.5 %all-to-all-start.4 = ((bf16[128,2,128]{2,0,1:T(8,128)(2,1)}), bf16[128,2,128]{2,0,1:T(8,128)(2,1)S(1)}, u32[]{:S(2)}, u32[]{:S(2)}) async-start(bf16[128,2,128]{2,0,1:T(8,128)(2,1)} %copy.81), calls=%async_computation.5 | async-start | bytes 131072 | tf_op jit(solution)/shard_map/all_to_all | solution.py:144
Sparse Core Ops, SparseCore 0:
  111.0 17.3 reduce-scatter.6
  130.9 25.2 reduce-scatter.4
where the time goes:
time: 166 us; the launch traced here: 165 us
  blocking collectives  52.4 us (32%)
  waiting for transfers between devices  34.3 us (21%)
  starting transfers between devices  19.8 us (12%)
  matrix products  18.4 us (11%)
  other arithmetic  15.3 us (9%)
  between operations  14.4 us (9%)
  local copies, waits for them, and re-layouts  10.2 us (6%)
    reduce_scatter x1, waiting for transfers between devices, body(): lax.psum_scatter(cache_numer, 'ctx', scatter_dimension=0, tiled=True)  26.9 us
    all_gather x1, blocking collectives, body(): value_piece = lax.all_gather(local_values, 'ctx', axis=0, tiled=True)  14.4 us
    all_gather x1, blocking collectives, body(): key_piece = lax.all_gather(local_keys, 'ctx', axis=0, tiled=True)  14.1 us
    pmax x1, blocking collectives, body(): global_top = lax.pmax(cache_top, 'ctx')  12.3 us
    all_gather x1, blocking collectives, body(): place_piece = lax.all_gather(token_pos, 'ctx', axis=0, tiled=True)  11.6 us
    dot_general x2, matrix products, attend(): jnp.einsum('qd,kd->qk', query_rows, key_block, preferred_element_type=jnp...  7.44 us
    reduce_sum x2, other arithmetic, online_step(): new_mass = old_mass * factor + jnp.sum(weights, axis=1)  6.93 us
    all_to_all x1, starting transfers between devices, body(): lax.all_to_all(jnp.take(page_scales, inverse, axis=0).astype(jnp.bfloat16...  6.32 us
  transfers between devices with their start and end apart: 7, of which 4 were waited for; matrix products, arithmetic and copies ran while one was open for 24% of the time, Pallas kernels for 0%

commit v1 on v0

v1 whole, which is shorter than its diff:
```python
import functools

import jax
import jax.numpy as jnp
from jax import lax
from jax.experimental import pallas as pl
from jax.experimental.pallas import tpu as pltpu
from jax.sharding import PartitionSpec as P

NEG_FILL = -1e30
FP_LIMIT = 448.0
LOG_TWO_E = 1.4426950408889634
META = 16
F32 = jnp.float32
BF16 = jnp.bfloat16
MESH = pl.DeviceIdType.MESH


def iota(shape, dim):
    return lax.broadcasted_iota(jnp.int32, shape, dim)


def dot(a, b):
    return lax.dot_general(a, b, (((1,), (0,)), ((), ())), preferred_element_type=F32)


def dot_t(a, b):
    return lax.dot_general(a, b, (((1,), (1,)), ((), ())), preferred_element_type=F32)


def one_hot(flag):
    return jnp.where(flag, F32(1.0), F32(0.0)).astype(BF16)


def tiled(array, width):
    return jnp.concatenate([array] * (width // array.shape[1]), axis=1)


def kernel(
    shards, sides, tok, groups, draft_rows, block,
    pos_ref, scale_ref, owner_ref, parents_ref,
    q_hbm, k_hbm, v_hbm, dq_hbm, dk_hbm, dv_hbm,
    out_ref, ck_ref, cv_ref, verify_ref,
    qbuf, kbuf, vbuf, tkbuf, tvbuf, mbuf, abuf, pbuf, accbuf, ckbuf, cvbuf, treebuf,
    local_sem, send_sem, recv_sem, tsend_sem, trecv_sem,
):
    me = lax.axis_index("ctx")
    my_side = lax.axis_index("side")
    width = qbuf.shape[1]
    half = tok // 2
    page = tok // shards
    share = draft_rows // shards
    tok_q = tok * groups
    own_q = share * groups
    scale = F32(LOG_TWO_E * width ** (-0.5))
    has_up = me + 1 < shards
    has_down = me > 0

    own_first = pl.multiple_of(me * own_q, own_q)
    copies = [
        pltpu.make_async_copy(k_hbm, kbuf.at[me, pl.ds(0, tok)], local_sem.at[0]),
        pltpu.make_async_copy(v_hbm, vbuf.at[me], local_sem.at[1]),
        pltpu.make_async_copy(dk_hbm, tkbuf.at[my_side], local_sem.at[2]),
        pltpu.make_async_copy(dv_hbm, tvbuf.at[my_side], local_sem.at[3]),
        pltpu.make_async_copy(q_hbm, qbuf.at[pl.ds(0, tok_q)], local_sem.at[4]),
        pltpu.make_async_copy(
            dq_hbm.at[pl.ds(own_first, own_q)], qbuf.at[pl.ds(tok_q, own_q)], local_sem.at[5]
        ),
    ]
    for copy in copies:
        copy.start()

    barrier = pltpu.get_barrier_semaphore()

    @pl.when(has_up)
    def _():
        pl.semaphore_signal(barrier, inc=1, device_id={"ctx": me + 1}, device_id_type=MESH)

    @pl.when(has_down)
    def _():
        pl.semaphore_signal(barrier, inc=1, device_id={"ctx": me - 1}, device_id_type=MESH)

    for step in range(1, sides):
        pl.semaphore_signal(
            barrier,
            inc=1,
            device_id={"side": lax.rem(my_side + step, sides)},
            device_id_type=MESH,
        )

    lane = iota((1, width), 1)
    rows = [jnp.zeros((1, width), F32) for _ in range(3)]
    for j in range(scale_ref.shape[1]):
        for i in range(2):
            e = scale_ref[i, j]
            bound = jnp.where(
                e == -7,
                F32(FP_LIMIT / 128),
                jnp.where(e == -6, F32(FP_LIMIT / 64), F32(FP_LIMIT / 32)),
            )
            rows[i] = jnp.where(lane == j, bound, rows[i])
        rows[2] = jnp.where(lane == j, owner_ref[j].astype(F32), rows[2])
    runs = [(pos_ref[i * half] // half).astype(F32) for i in range(2)]
    place = iota((META, width), 0)
    meta = jnp.zeros((META, width), F32)
    for i in range(3):
        meta = jnp.where(place == i, rows[i], meta)
    for i in range(2):
        meta = jnp.where(place == 3 + i, runs[i], meta)
    kbuf[me, pl.ds(tok, META), :] = meta.astype(BF16)

    def link(kind, shard, up):
        buf = (kbuf, vbuf)[kind]
        return pltpu.make_async_remote_copy(
            src_ref=buf.at[shard],
            dst_ref=buf.at[shard],
            send_sem=send_sem.at[kind, int(up), shard],
            recv_sem=recv_sem.at[kind, shard],
            device_id={"ctx": me + 1 if up else me - 1},
            device_id_type=MESH,
        )

    def arrive(kind, step):
        below, above = me - step, me + step

        @pl.when(below >= 0)
        def _():
            link(kind, below, False).wait_recv()

            @pl.when(has_up)
            def _():
                link(kind, below, True).start()

        @pl.when(above < shards)
        def _():
            link(kind, above, True).wait_recv()

            @pl.when(has_down)
            def _():
                link(kind, above, False).start()

    copies[0].wait()
    copies[1].wait()
    count = has_up.astype(jnp.int32) + has_down.astype(jnp.int32) + (sides - 1)
    pl.semaphore_wait(barrier, count)
    for kind in range(2):

        @pl.when(has_up)
        def _():
            link(kind, me, True).start()

        @pl.when(has_down)
        def _():
            link(kind, me, False).start()

    copies[2].wait()
    copies[3].wait()
    tree_sends = []
    for step in range(1, sides):
        for kind, buf in enumerate((tkbuf, tvbuf)):
            send = pltpu.make_async_remote_copy(
                src_ref=buf.at[my_side],
                dst_ref=buf.at[my_side],
                send_sem=tsend_sem.at[kind, step],
                recv_sem=trecv_sem.at[kind, step],
                device_id={"side": lax.rem(my_side + step, sides)},
                device_id_type=MESH,
            )
            send.start()
            tree_sends.append(send)

    q_row, q_col = iota((draft_rows, draft_rows), 0), iota((draft_rows, draft_rows), 1)
    tree = one_hot((parents_ref[...] == q_row) | (q_row == q_col))
    for _ in range((draft_rows - 1).bit_length()):
        tree = one_hot(dot(tree, tree) > 0.5)
    side_keys = tkbuf.shape[1]
    tree_keys = sides * side_keys
    mine = one_hot(
        iota((own_q, draft_rows), 1) == me * share + iota((own_q, draft_rows), 0) // groups
    )
    column = iota((draft_rows, tree_keys), 1)
    inside = column % side_keys
    source = (column // side_keys) * (side_keys // sides) + inside // sides
    spread = one_hot((source == iota((draft_rows, tree_keys), 0)) & (inside % sides == my_side))
    treebuf[...] = dot(dot_t(mine, tree).astype(BF16), spread)

    if shards > 1:
        arrive(0, 1)
        arrive(1, 1)

    page_of = one_hot(iota((tok, width), 0) // page == iota((tok, width), 1))
    ones_sq = jnp.ones((width, width), BF16)
    ones_v = jnp.ones((tok, width), BF16)

    def clipped(data, meta_rows, which):
        bound = dot(page_of * meta_rows[which : which + 1, :], ones_sq)
        return jnp.clip(data.astype(F32), -bound, bound).astype(BF16)

    def keep(meta_rows, data, target, shard):
        owner = dot_t(meta_rows, page_of)[2:3, :]
        pick = one_hot(
            (owner == me.astype(F32)) & (iota((page, tok), 1) % page == iota((page, tok), 0))
        )
        target[pl.ds(pl.multiple_of(shard * page, page), page), :] = dot(pick, data)

    def run_bias(meta_rows, own):
        wide = meta_rows.astype(F32)
        key_runs = jnp.concatenate(
            [jnp.broadcast_to(wide[3 + i : 4 + i, :1], (1, half)) for i in range(2)], axis=1
        )
        return jnp.where(key_runs < runs[own], F32(0.0), F32(NEG_FILL))

    def weigh(at, keys, bias=None, allowed=None, first=False):
        scores = dot_t(qbuf[at, :], keys) * scale
        if bias is not None:
            scores = scores + bias
        if allowed is not None:
            scores = jnp.where(allowed, scores, F32(NEG_FILL))
        top = jnp.ceil(jnp.max(scores, axis=1, keepdims=True))
        factor = None
        if first:
            new_top = jnp.broadcast_to(top, (block, width))
        else:
            old_top = mbuf[at, :]
            new_top = jnp.maximum(old_top, top)
            factor = jnp.exp2(old_top - new_top)
        mbuf[at, :] = new_top
        weights = jnp.exp2(scores - tiled(new_top, scores.shape[1])).astype(BF16)
        return factor, weights

    def add(at, factor, weights, values):
        part = dot(weights, values)
        if factor is None:
            accbuf[at, :] = part
        else:
            accbuf[at, :] = accbuf[at, :] * tiled(factor, 2 * width) + part

    def each(first, total, run):
        @pl.loop(0, total // block)
        def _(i):
            run(i, pl.ds(pl.multiple_of(first + i * block, block), block))

    half_q = half * groups

    copies[4].wait()
    own_keys = kbuf[me, pl.ds(0, tok), :]
    own_meta = kbuf[me, pl.ds(tok, META), :]
    own_values = jnp.concatenate([vbuf[me], ones_v], axis=1)
    for part in range(2):
        bias = run_bias(own_meta, part)

        def own_block(i, at, part=part, bias=bias):
            key = iota((block, tok), 1)
            query = (i * block + iota((block, tok), 0)) // groups
            allowed = ((key // half == part) & (key - part * half <= query)) | (bias > -1.0)
            factor, weights = weigh(at, own_keys, allowed=allowed, first=True)
            add(at, factor, weights, own_values)

        each(part * half_q, half_q, own_block)

    copies[5].wait()
    cache_k = clipped(own_keys, own_meta, 0)
    cache_v = clipped(vbuf[me], own_meta, 1)
    keep(own_meta, cache_k, ckbuf, me)
    keep(own_meta, cache_v, cvbuf, me)
    cache_v1 = jnp.concatenate([cache_v, ones_v], axis=1)

    def own_verify(i, at):
        factor, weights = weigh(at, cache_k, first=True)
        add(at, factor, weights, cache_v1)

    each(tok_q, own_q, own_verify)

    for send in tree_sends:
        send.wait_recv()
    all_tk = tkbuf[...].reshape(tree_keys, width)
    all_tv = jnp.concatenate(
        [tvbuf[...].reshape(tree_keys, width), jnp.ones((tree_keys, width), BF16)], axis=1
    )

    def tree_verify(i, at):
        allowed = treebuf[pl.ds(pl.multiple_of(i * block, block), block), :] > 0.5
        factor, weights = weigh(at, all_tk, allowed=allowed)
        add(at, factor, weights, all_tv)

    each(tok_q, own_q, tree_verify)

    def scores_of(shard, slot):
        keys = kbuf[shard, pl.ds(0, tok), :]
        meta_rows = kbuf[shard, pl.ds(tok, META), :]

        def run(i, at, keys=keys, bias=None):
            factor, weights = weigh(at, keys, bias=bias)
            abuf[slot, at, :] = factor
            pbuf[slot, at, :] = weights

        for part in range(2):
            each(part * half_q, half_q, functools.partial(run, bias=run_bias(meta_rows, part)))
        far_k = clipped(keys, meta_rows, 0)
        keep(meta_rows, far_k, ckbuf, shard)
        each(tok_q, own_q, functools.partial(run, keys=far_k))

    def values_of(shard, slot):
        values = vbuf[shard]
        meta_rows = kbuf[shard, pl.ds(tok, META), :]

        def run(i, at, values):
            add(at, abuf[slot, at, :], pbuf[slot, at, :], values)

        wide = jnp.concatenate([values, ones_v], axis=1)
        each(0, tok_q, functools.partial(run, values=wide))
        far_v = clipped(values, meta_rows, 1)
        keep(meta_rows, far_v, cvbuf, shard)
        far_v1 = jnp.concatenate([far_v, ones_v], axis=1)
        each(tok_q, own_q, functools.partial(run, values=far_v1))

    def both(step, run):
        @pl.loop(0, 2)
        def _(slot):
            shard = me + step * (2 * slot - 1)

            @pl.when((shard >= 0) & (shard < shards))
            def _():
                run(shard, slot)

    @pl.loop(1, shards)
    def _(step):
        both(step, scores_of)

        @pl.when(step > 1)
        def _():
            arrive(1, step)

        both(step, values_of)

        @pl.when(step + 1 < shards)
        def _():
            arrive(0, step + 1)

    def finish(target, first):
        def run(i, at):
            total = accbuf[at, :]
            to = pl.ds(pl.multiple_of(i * block, block), block)
            target[to, :] = (total[:, :width] / total[:, width:]).astype(BF16)

        return run

    each(0, tok_q, finish(out_ref, 0))
    each(tok_q, own_q, finish(verify_ref, tok_q))
    ck_ref[...] = ckbuf[...].astype(BF16)
    cv_ref[...] = cvbuf[...].astype(BF16)

    for send in tree_sends:
        send.wait_send()

    @pl.loop(0, shards)
    def _(step):
        below, above = me - step, me + step
        for kind in range(2):

            @pl.when((below >= 0) & has_up)
            def _():
                link(kind, below, True).wait_send()

            @pl.when((above < shards) & has_down)
            def _():
                link(kind, above, False).wait_send()


def body(
    shards, sides,
    prefill_query, prefill_keys, prefill_values, token_pos, scale_exp, page_owner,
    draft_query, draft_keys, draft_values, parents,
):
    tok, groups, width = prefill_query.shape
    draft_rows = draft_query.shape[0]
    own_q = draft_rows // shards * groups
    all_q = tok * groups + own_q
    side_keys = draft_keys.shape[0] * draft_keys.shape[1]
    block = min(256, own_q)
    hbm = pl.BlockSpec(memory_space=pl.ANY)
    smem = pl.BlockSpec(memory_space=pltpu.SMEM)
    vmem = pl.BlockSpec(memory_space=pltpu.VMEM)
    out, ck, cv, verify = pl.pallas_call(
        functools.partial(kernel, shards, sides, tok, groups, draft_rows, block),
        out_shape=(
            jax.ShapeDtypeStruct((tok * groups, width), BF16),
            jax.ShapeDtypeStruct((tok, width), BF16),
            jax.ShapeDtypeStruct((tok, width), BF16),
            jax.ShapeDtypeStruct((own_q, width), BF16),
        ),
        in_specs=[smem, smem, smem, vmem] + [hbm] * 6,
        out_specs=(vmem, vmem, vmem, vmem),
        scratch_shapes=[
            pltpu.VMEM((all_q, width), BF16),
            pltpu.VMEM((shards, tok + META, width), BF16),
            pltpu.VMEM((shards, tok, width), BF16),
            pltpu.VMEM((sides, side_keys, width), BF16),
            pltpu.VMEM((sides, side_keys, width), BF16),
            pltpu.VMEM((all_q, width), F32),
            pltpu.VMEM((2, all_q, width), F32),
            pltpu.VMEM((2, all_q, tok), BF16),
            pltpu.VMEM((all_q, 2 * width), F32),
            pltpu.VMEM((tok, width), F32),
            pltpu.VMEM((tok, width), F32),
            pltpu.VMEM((own_q, sides * side_keys), F32),
            pltpu.SemaphoreType.DMA((6,)),
            pltpu.SemaphoreType.DMA((2, 2, shards)),
            pltpu.SemaphoreType.DMA((2, shards)),
            pltpu.SemaphoreType.DMA((2, sides)),
            pltpu.SemaphoreType.DMA((2, sides)),
        ],
        compiler_params=pltpu.CompilerParams(
            collective_id=0, has_side_effects=True, vmem_limit_bytes=48 * 1024 * 1024
        ),
    )(
        token_pos,
        jnp.transpose(scale_exp[:, 0, :]),
        page_owner,
        parents.reshape(1, draft_rows),
        prefill_query.reshape(tok * groups, width),
        prefill_keys.reshape(tok, width),
        prefill_values.reshape(tok, width),
        draft_query.reshape(draft_rows * groups, width),
        draft_keys.reshape(side_keys, width),
        draft_values.reshape(side_keys, width),
    )
    return (
        out.reshape(tok, groups, width),
        ck.reshape(tok, 1, width),
        cv.reshape(tok, 1, width),
        verify.reshape(draft_rows // shards, groups, width),
    )


def solution(mesh):
    head_spec = P("ctx", ("head", "side"), None)
    return jax.shard_map(
        functools.partial(body, mesh.shape["ctx"], mesh.shape["side"]),
        mesh=mesh,
        in_specs=(
            head_spec,
            head_spec,
            head_spec,
            P("ctx"),
            head_spec,
            P("ctx"),
            P(None, ("head", "side"), None),
            P("side", "head", None),
            P("side", "head", None),
            P(),
        ),
        out_specs=(head_spec,) * 4,
        check_vma=False,
    )
```

time: 166 us -> 46 us (0.28)
  blocking collectives: 52.4 us -> 0 us
  Pallas kernels: 0 us -> 36.1 us
  waiting for transfers between devices: 34.3 us -> 0 us
  starting transfers between devices: 19.8 us -> 0 us
  matrix products: 18.4 us -> 0 us
  other arithmetic: 15.3 us -> 0 us
  between operations: 14.4 us -> 0.68 us
    all_gather x3 -> x0, blocking collectives: 40.1 us -> none  [the longest x1 14.4 us: body(): value_piece = lax.all_gather(local_values, 'ctx', axis=0, tiled=True)]
    pallas_call x0 -> x1, Pallas kernels: none -> 36.1 us  [body(): pl.pallas_call(functools.partial(kernel, shards, sides, tok, groups, draf...]
    reduce_scatter x1 -> x0, waiting for transfers between devices: 26.9 us -> none  [body(): lax.psum_scatter(cache_numer, 'ctx', scatter_dimension=0, tiled=True)]
    all_to_all x5 -> x0, starting transfers between devices: 19.7 us -> none  [the longest x1 6.32 us: body(): lax.all_to_all(jnp.take(page_scales, inverse, axis=0).astype(jnp.bfloat16...]
    dot_general x17 -> x0, matrix products: 18.4 us -> none  [the longest x2 7.44 us: attend(): jnp.einsum('qd,kd->qk', query_rows, key_block, preferred_element_type=jnp...]
    pmax x1 -> x0, blocking collectives: 12.3 us -> none  [body(): global_top = lax.pmax(cache_top, 'ctx')]
    reduce_sum x6 -> x0, other arithmetic: 11.8 us -> none  [the longest x2 6.93 us: online_step(): new_mass = old_mass * factor + jnp.sum(weights, axis=1)]
    all_to_all x5 -> x0, waiting for transfers between devices: 6.79 us -> none  [the longest x1 5.59 us: body(): lax.all_to_all(jnp.take(scaled_keys, inverse, axis=0), 'ctx', split_axis=...]
  transfers between devices with their start and end apart: 7 -> 0, of which waited for: 4 -> 0; matrix products, arithmetic and copies ran while one was open for 24% -> 0% of each run, Pallas kernels for 0% -> 0%
where the time goes in v1:
time: 46 us; the launch traced here: 45.6 us
  Pallas kernels  36.1 us (78%)
  local copies, waits for them, and re-layouts  8.83 us (19%)
  between operations  0.68 us (1%)
    pallas_call x1, Pallas kernels, body(): pl.pallas_call(functools.partial(kernel, shards, sides, tok, groups, draf...  36.1 us
    unnamed x24, local copies, waits for them, and re-layouts  8.83 us

profile of v1, /device:TPU:0, one launch (start us, length us, event | category | flops | bytes accessed | tf_op | source)
XLA Modules:
  0.0 45.6 jit_solution(13960070105273731841)
XLA Ops:
  0.6 0.0 copy-start.7
  0.6 0.0 copy-start.8
  0.7 0.0 copy-start.6
  0.7 0.0 copy-start.9
  0.7 0.6 %copy-done.7 = s32[4,1,2]{0,2,1:T(2,128)S(1)} copy-done((s32[4,1,2]{0,2,1:T(2,128)S(1)}, s32[4,1,2]{0,2,1:T(2,128)}, u32[]{:S(2)}) %copy-start.7) | copy-done | bytes 56
  1.3 0.0 copy-done.8
  1.3 0.0 copy-done.6
  1.3 0.0 copy-done.9
  1.3 0.0 copy-start
  1.4 1.0 %copy-done = bf16[256,8,128]{2,1,0:T(8,128)(2,1)S(1)} copy-done((bf16[256,8,128]{2,1,0:T(8,128)(2,1)S(1)}, bf16[256,8,128]{2,1,0:T(8,128)(2,1)}, u32[]{:S(2)}) %copy-start) | copy-done | bytes 524312
  2.4 0.0 copy-start.1
  2.4 1.0 %copy-done.1 = bf16[256,8,128]{2,1,0:T(8,128)(2,1)S(1)} copy-done((bf16[256,8,128]{2,1,0:T(8,128)(2,1)S(1)}, bf16[256,8,128]{2,1,0:T(8,128)(2,1)}, u32[]{:S(2)}) %copy-start.1) | copy-done | bytes 524312
  3.4 0.0 copy-start.2
  3.4 0.8 %copy-done.2 = bf16[256,1,128]{2,0,1:T(8,128)(2,1)S(1)} copy-done((bf16[256,1,128]{2,0,1:T(8,128)(2,1)S(1)}, bf16[256,1,128]{2,0,1:T(8,128)(2,1)}, u32[]{:S(2)}) %copy-start.2) | copy-done | bytes 65560
  4.3 0.0 copy-start.3
  4.3 0.8 %copy-done.3 = bf16[256,1,128]{2,0,1:T(8,128)(2,1)S(1)} copy-done((bf16[256,1,128]{2,0,1:T(8,128)(2,1)S(1)}, bf16[256,1,128]{2,0,1:T(8,128)(2,1)}, u32[]{:S(2)}) %copy-start.3) | copy-done | bytes 65560
  5.1 0.0 copy-start.4
  5.1 0.8 %copy-done.4 = bf16[128,2,128]{2,1,0:T(2,128)(2,1)S(1)} copy-done((bf16[128,2,128]{2,1,0:T(2,128)(2,1)S(1)}, bf16[128,2,128]{2,1,0:T(2,128)(2,1)}, u32[]{:S(2)}) %copy-start.4) | copy-done | bytes 65560
  6.0 0.0 copy-start.5
  6.0 0.8 %copy-done.5 = bf16[128,2,128]{2,1,0:T(2,128)(2,1)S(1)} copy-done((bf16[128,2,128]{2,1,0:T(2,128)(2,1)S(1)}, bf16[128,2,128]{2,1,0:T(2,128)(2,1)}, u32[]{:S(2)}) %copy-start.5) | copy-done | bytes 65560
  6.8 36.1 %shard_map.129 = (bf16[2048,128]{1,0:T(8,128)(2,1)S(1)}, bf16[256,128]{1,0:T(8,128)(2,1)S(1)}, bf16[256,128]{1,0:T(8,128)(2,1)S(1)}, bf16[512,128]{1,0:T(8,128)(2,1)S(1)}) custom-call(s32[256]{0:T(256)S(1)} %copy-done.6, s32[2,4]{1,0:T(2,128)S(1)} %bitcast.24, s32[4]{0:T(128)S(1)} %copy-done.9, s32[1,256]{1,0:T(1,128)S(1)} %bitcast.25, ...), custom_call_target="tpu_custom_call" | custom-call | tf_op jit(solution)/shard_map/pallas_call | solution.py:384
  42.9 0.8 %copy.18 = bf16[256,8,128]{2,1,0:T(8,128)(2,1)} copy(bf16[256,8,128]{2,1,0:T(8,128)(2,1)S(1)} %bitcast.16) | data formatting | bytes 1048576
  43.7 0.6 %copy.19 = bf16[256,1,128]{2,0,1:T(8,128)(2,1)} copy(bf16[256,1,128]{2,0,1:T(8,128)(2,1)S(1)} %bitcast.23) | data formatting | bytes 131072
  44.3 0.6 %copy.20 = bf16[256,1,128]{2,0,1:T(8,128)(2,1)} copy(bf16[256,1,128]{2,0,1:T(8,128)(2,1)S(1)} %bitcast.22) | data formatting | bytes 131072
  45.0 0.7 %copy.21 = bf16[64,8,128]{2,1,0:T(8,128)(2,1)} copy(bf16[64,8,128]{2,1,0:T(8,128)(2,1)S(1)} %bitcast.17) | data formatting | bytes 262144
Async XLA Ops:
  0.6 0.7 %copy-start.7 = (s32[4,1,2]{0,2,1:T(2,128)S(1)}, s32[4,1,2]{0,2,1:T(2,128)}, u32[]{:S(2)}) copy-start(s32[4,1,2]{0,2,1:T(2,128)} %param.14) | copy-start | bytes 100
  0.6 0.7 %copy-start.8 = (s32[256]{0:T(256)S(1)}, s32[256]{0:T(256)}, u32[]{:S(2)}) copy-start(s32[256]{0:T(256)} %param.19) | copy-start | bytes 3076
  0.7 0.7 %copy-start.6 = (s32[256]{0:T(256)S(1)}, s32[256]{0:T(256)}, u32[]{:S(2)}) copy-start(s32[256]{0:T(256)} %pos_ref.1) | copy-start | bytes 3076
  0.7 0.7 %copy-start.9 = (s32[4]{0:T(128)S(1)}, s32[4]{0:T(128)}, u32[]{:S(2)}) copy-start(s32[4]{0:T(128)} %owner_ref.1) | copy-start | bytes 52
  1.3 1.0 %copy-start = (bf16[256,8,128]{2,1,0:T(8,128)(2,1)S(1)}, bf16[256,8,128]{2,1,0:T(8,128)(2,1)}, u32[]{:S(2)}) copy-start(bf16[256,8,128]{2,1,0:T(8,128)(2,1)} %param.10) | copy-start | bytes 1572868
  2.4 1.0 %copy-start.1 = (bf16[256,8,128]{2,1,0:T(8,128)(2,1)S(1)}, bf16[256,8,128]{2,1,0:T(8,128)(2,1)}, u32[]{:S(2)}) copy-start(bf16[256,8,128]{2,1,0:T(8,128)(2,1)} %param.16) | copy-start | bytes 1572868
  3.4 0.8 %copy-start.2 = (bf16[256,1,128]{2,0,1:T(8,128)(2,1)S(1)}, bf16[256,1,128]{2,0,1:T(8,128)(2,1)}, u32[]{:S(2)}) copy-start(bf16[256,1,128]{2,0,1:T(8,128)(2,1)} %param.11) | copy-start | bytes 196612
  4.3 0.8 %copy-start.3 = (bf16[256,1,128]{2,0,1:T(8,128)(2,1)S(1)}, bf16[256,1,128]{2,0,1:T(8,128)(2,1)}, u32[]{:S(2)}) copy-start(bf16[256,1,128]{2,0,1:T(8,128)(2,1)} %param.12) | copy-start | bytes 196612
  5.1 0.8 %copy-start.4 = (bf16[128,2,128]{2,1,0:T(2,128)(2,1)S(1)}, bf16[128,2,128]{2,1,0:T(2,128)(2,1)}, u32[]{:S(2)}) copy-start(bf16[128,2,128]{2,1,0:T(2,128)(2,1)} %param.17) | copy-start | bytes 196612
  6.0 0.8 %copy-start.5 = (bf16[128,2,128]{2,1,0:T(2,128)(2,1)S(1)}, bf16[128,2,128]{2,1,0:T(2,128)(2,1)}, u32[]{:S(2)}) copy-start(bf16[128,2,128]{2,1,0:T(2,128)(2,1)} %param.18) | copy-start | bytes 196612

commit v2 on v1

--- a/solution.py
+++ b/solution.py
@@ -236,9 +236,8 @@
             accbuf[at, :] = accbuf[at, :] * tiled(factor, 2 * width) + part
 
     def each(first, total, run):
-        @pl.loop(0, total // block)
-        def _(i):
-            run(i, pl.ds(pl.multiple_of(first + i * block, block), block))
+        for i in range(total // block):
+            run(i, pl.ds(first + i * block, block))
 
     half_q = half * groups
 
@@ -279,7 +278,7 @@
     )
 
     def tree_verify(i, at):
-        allowed = treebuf[pl.ds(pl.multiple_of(i * block, block), block), :] > 0.5
+        allowed = treebuf[pl.ds(i * block, block), :] > 0.5
         factor, weights = weigh(at, all_tk, allowed=allowed)
         add(at, factor, weights, all_tv)
 
@@ -337,16 +336,12 @@
         def _():
             arrive(0, step + 1)
 
-    def finish(target, first):
-        def run(i, at):
-            total = accbuf[at, :]
-            to = pl.ds(pl.multiple_of(i * block, block), block)
-            target[to, :] = (total[:, :width] / total[:, width:]).astype(BF16)
-
-        return run
-
-    each(0, tok_q, finish(out_ref, 0))
-    each(tok_q, own_q, finish(verify_ref, tok_q))
+    def finish(i, at, target):
+        total = accbuf[at, :]
+        target[pl.ds(i * block, block), :] = (total[:, :width] / total[:, width:]).astype(BF16)
+
+    each(0, tok_q, functools.partial(finish, target=out_ref))
+    each(tok_q, own_q, functools.partial(finish, target=verify_ref))
     ck_ref[...] = ckbuf[...].astype(BF16)
     cv_ref[...] = cvbuf[...].astype(BF16)
 
@@ -378,7 +373,7 @@
     all_q = tok * groups + own_q
     side_keys = draft_keys.shape[0] * draft_keys.shape[1]
     block = min(256, own_q)
-    hbm = pl.BlockSpec(memory_space=pl.ANY)
+    hbm = pl.BlockSpec(memory_space=pltpu.HBM)
     smem = pl.BlockSpec(memory_space=pltpu.SMEM)
     vmem = pl.BlockSpec(memory_space=pltpu.VMEM)
     out, ck, cv, verify = pl.pallas_call(
@@ -411,7 +406,7 @@
             pltpu.SemaphoreType.DMA((2, sides)),
         ],
         compiler_params=pltpu.CompilerParams(
-            collective_id=0, has_side_effects=True, vmem_limit_bytes=48 * 1024 * 1024
+            collective_id=0, has_side_effects=True, vmem_limit_bytes=63 * 1024 * 1024
         ),
     )(
         token_pos,

time: 46 us -> 26.3 us (0.57)
  Pallas kernels: 36.1 us -> 21.7 us
  local copies, waits for them, and re-layouts: 8.83 us -> 3.83 us
    pallas_call x1, Pallas kernels: 36.1 us -> 21.7 us  [body(): pl.pallas_call(functools.partial(kernel, shards, sides, tok, groups, draf...]
    unnamed x24 -> x10, local copies, waits for them, and re-layouts: 8.83 us -> 3.83 us
where the time goes in v2:
time: 26.3 us; the launch traced here: 26.2 us
  Pallas kernels  21.7 us (83%)
  local copies, waits for them, and re-layouts  3.83 us (15%)
  between operations  0.66 us (3%)
    pallas_call x1, Pallas kernels, body(): pl.pallas_call(functools.partial(kernel, shards, sides, tok, groups, draf...  21.7 us
    unnamed x10, local copies, waits for them, and re-layouts  3.83 us

profile of v2, /device:TPU:0, one launch (start us, length us, event | category | flops | bytes accessed | tf_op | source)
XLA Modules:
  0.0 26.2 jit_solution(2941748661332150323)
XLA Ops:
  0.6 21.7 %shard_map.129 = (bf16[2048,128]{1,0:T(8,128)(2,1)}, bf16[256,128]{1,0:T(8,128)(2,1)}, bf16[256,128]{1,0:T(8,128)(2,1)}, bf16[512,128]{1,0:T(8,128)(2,1)}) custom-call(s32[256]{0:T(256)} %pos_ref.1, s32[2,4]{1,0:T(2,128)} %bitcast.24, s32[4]{0:T(128)} %owner_ref.1, s32[1,256]{1,0:T(1,128)} %bitcast.25, bf16[2048,128]{1,0:T(8,128)(2,1)} %bitcast.14, ...), custom_call_target="tpu_custom_call" | custom-call | tf_op jit(solution)/shard_map/pallas_call | solution.py:379
  22.3 0.0 copy-start.2
  22.3 0.0 copy-start.1
  22.3 1.9 %copy.18 = bf16[256,8,128]{2,1,0:T(8,128)(2,1)} copy(bf16[256,8,128]{2,1,0:T(8,128)(2,1)} %bitcast.16) | data formatting | bytes 1048576
  24.2 0.0 copy-done.2
  24.2 0.0 copy-start
  24.2 0.6 %copy.19 = bf16[256,1,128]{2,0,1:T(8,128)(2,1)} copy(bf16[256,1,128]{2,0,1:T(8,128)(2,1)S(1)} %bitcast.23) | data formatting | bytes 131072
  24.9 0.0 copy-done.1
  24.9 0.6 %copy.20 = bf16[256,1,128]{2,0,1:T(8,128)(2,1)} copy(bf16[256,1,128]{2,0,1:T(8,128)(2,1)S(1)} %bitcast.22) | data formatting | bytes 131072
  25.5 0.0 copy-done
  25.5 0.7 %copy.21 = bf16[64,8,128]{2,1,0:T(8,128)(2,1)} copy(bf16[64,8,128]{2,1,0:T(8,128)(2,1)S(1)} %bitcast.17) | data formatting | bytes 262144
Async XLA Ops:
  22.3 1.9 %copy-start.2 = (bf16[256,128]{1,0:T(8,128)(2,1)S(1)}, bf16[256,128]{1,0:T(8,128)(2,1)}, u32[]{:S(2)}) copy-start(bf16[256,128]{1,0:T(8,128)(2,1)} %get-tuple-element.9) | copy-start | bytes 196612
  22.3 2.5 %copy-start.1 = (bf16[256,128]{1,0:T(8,128)(2,1)S(1)}, bf16[256,128]{1,0:T(8,128)(2,1)}, u32[]{:S(2)}) copy-start(bf16[256,128]{1,0:T(8,128)(2,1)} %get-tuple-element.10) | copy-start | bytes 196612
  24.2 1.3 %copy-start = (bf16[512,128]{1,0:T(8,128)(2,1)S(1)}, bf16[512,128]{1,0:T(8,128)(2,1)}, u32[]{:S(2)}) copy-start(bf16[512,128]{1,0:T(8,128)(2,1)} %get-tuple-element.11) | copy-start | bytes 393220

commit v3 on v2

--- a/solution.py
+++ b/solution.py
@@ -41,7 +41,7 @@
     pos_ref, scale_ref, owner_ref, parents_ref,
     q_hbm, k_hbm, v_hbm, dq_hbm, dk_hbm, dv_hbm,
     out_ref, ck_ref, cv_ref, verify_ref,
-    qbuf, kbuf, vbuf, tkbuf, tvbuf, mbuf, abuf, pbuf, accbuf, ckbuf, cvbuf, treebuf,
+    qbuf, kbuf, vbuf, tkbuf, tvbuf, mbuf, accbuf, ckbuf, cvbuf, treebuf,
     local_sem, send_sem, recv_sem, tsend_sem, trecv_sem,
 ):
     me = lax.axis_index("ctx")
@@ -284,57 +284,44 @@
 
     each(tok_q, own_q, tree_verify)
 
-    def scores_of(shard, slot):
+    def attend(shard):
         keys = kbuf[shard, pl.ds(0, tok), :]
         meta_rows = kbuf[shard, pl.ds(tok, META), :]
-
-        def run(i, at, keys=keys, bias=None):
+        values = vbuf[shard]
+
+        def run(i, at, keys, values, bias):
             factor, weights = weigh(at, keys, bias=bias)
-            abuf[slot, at, :] = factor
-            pbuf[slot, at, :] = weights
-
+            add(at, factor, weights, values)
+
+        wide = jnp.concatenate([values, ones_v], axis=1)
         for part in range(2):
-            each(part * half_q, half_q, functools.partial(run, bias=run_bias(meta_rows, part)))
+            bias = run_bias(meta_rows, part)
+            each(
+                part * half_q,
+                half_q,
+                functools.partial(run, keys=keys, values=wide, bias=bias),
+            )
         far_k = clipped(keys, meta_rows, 0)
+        far_v = clipped(values, meta_rows, 1)
         keep(meta_rows, far_k, ckbuf, shard)
-        each(tok_q, own_q, functools.partial(run, keys=far_k))
-
-    def values_of(shard, slot):
-        values = vbuf[shard]
-        meta_rows = kbuf[shard, pl.ds(tok, META), :]
-
-        def run(i, at, values):
-            add(at, abuf[slot, at, :], pbuf[slot, at, :], values)
-
-        wide = jnp.concatenate([values, ones_v], axis=1)
-        each(0, tok_q, functools.partial(run, values=wide))
-        far_v = clipped(values, meta_rows, 1)
         keep(meta_rows, far_v, cvbuf, shard)
         far_v1 = jnp.concatenate([far_v, ones_v], axis=1)
-        each(tok_q, own_q, functools.partial(run, values=far_v1))
-
-    def both(step, run):
+        each(tok_q, own_q, functools.partial(run, keys=far_k, values=far_v1, bias=None))
+
+    @pl.loop(1, shards)
+    def _(step):
+        @pl.when(step + 1 < shards)
+        def _():
+            arrive(0, step + 1)
+            arrive(1, step + 1)
+
         @pl.loop(0, 2)
         def _(slot):
             shard = me + step * (2 * slot - 1)
 
             @pl.when((shard >= 0) & (shard < shards))
             def _():
-                run(shard, slot)
-
-    @pl.loop(1, shards)
-    def _(step):
-        both(step, scores_of)
-
-        @pl.when(step > 1)
-        def _():
-            arrive(1, step)
-
-        both(step, values_of)
-
-        @pl.when(step + 1 < shards)
-        def _():
-            arrive(0, step + 1)
+                attend(shard)
 
     def finish(i, at, target):
         total = accbuf[at, :]
@@ -360,6 +347,11 @@
             @pl.when((above < shards) & has_down)
             def _():
                 link(kind, above, False).wait_send()
+
+
+def hand_over(*refs):
+    for source, target in zip(refs[:4], refs[4:]):
+        target[...] = source[...]
 
 
 def body(
@@ -393,8 +385,6 @@
             pltpu.VMEM((sides, side_keys, width), BF16),
             pltpu.VMEM((sides, side_keys, width), BF16),
             pltpu.VMEM((all_q, width), F32),
-            pltpu.VMEM((2, all_q, width), F32),
-            pltpu.VMEM((2, all_q, tok), BF16),
             pltpu.VMEM((all_q, 2 * width), F32),
             pltpu.VMEM((tok, width), F32),
             pltpu.VMEM((tok, width), F32),
@@ -420,6 +410,12 @@
         draft_keys.reshape(side_keys, width),
         draft_values.reshape(side_keys, width),
     )
+    out, ck, cv, verify = pl.pallas_call(
+        hand_over,
+        out_shape=tuple(jax.ShapeDtypeStruct(x.shape, x.dtype) for x in (out, ck, cv, verify)),
+        in_specs=[vmem] * 4,
+        out_specs=(vmem,) * 4,
+    )(out, ck, cv, verify)
     return (
         out.reshape(tok, groups, width),
         ck.reshape(tok, 1, width),

time: 26.3 us -> 23.4 us (0.89)
  local copies, waits for them, and re-layouts: 3.83 us -> 0 us
  Pallas kernels: 21.7 us -> 22.6 us
    unnamed x10 -> x0, local copies, waits for them, and re-layouts: 3.83 us -> none
    pallas_call x0 -> x1, Pallas kernels: none -> 2.01 us  [body(): pl.pallas_call(hand_over, out_shape=tuple((jax.ShapeDtypeStruct(x.shape,...]
    pallas_call x1, Pallas kernels: 21.7 us -> 20.6 us  [body(): pl.pallas_call(functools.partial(kernel, shards, sides, tok, groups, draf...]
where the time goes in v3:
time: 23.4 us; the launch traced here: 23.2 us
  Pallas kernels  22.6 us (97%)
  between operations  0.64 us (3%)
    pallas_call x1, Pallas kernels, body(): pl.pallas_call(functools.partial(kernel, shards, sides, tok, groups, draf...  20.6 us
    pallas_call x1, Pallas kernels, body(): pl.pallas_call(hand_over, out_shape=tuple((jax.ShapeDtypeStruct(x.shape,...  2.01 us

profile of v3, /device:TPU:0, one launch (start us, length us, event | category | flops | bytes accessed | tf_op | source)
XLA Modules:
  0.0 23.2 jit_solution(8673215251793579757)
XLA Ops:
  0.6 20.6 %shard_map.129 = (bf16[2048,128]{1,0:T(8,128)(2,1)}, bf16[256,128]{1,0:T(8,128)(2,1)}, bf16[256,128]{1,0:T(8,128)(2,1)}, bf16[512,128]{1,0:T(8,128)(2,1)}) custom-call(s32[256]{0:T(256)} %pos_ref.1, s32[2,4]{1,0:T(2,128)} %bitcast.20, s32[4]{0:T(128)} %owner_ref.1, s32[1,256]{1,0:T(1,128)} %bitcast.21, bf16[2048,128]{1,0:T(8,128)(2,1)} %bitcast.14, ...), custom_call_target="tpu_custom_call" | custom-call | tf_op jit(solution)/shard_map/pallas_call | solution.py:371
  21.2 2.0 %shard_map.130 = (bf16[2048,128]{1,0:T(8,128)(2,1)}, bf16[256,128]{1,0:T(8,128)(2,1)}, bf16[256,128]{1,0:T(8,128)(2,1)}, bf16[512,128]{1,0:T(8,128)(2,1)}) custom-call(bf16[2048,128]{1,0:T(8,128)(2,1)} %get-tuple-element.12.refs_0_, bf16[256,128]{1,0:T(8,128)(2,1)} %get-tuple-element.13.refs_1_, bf16[256,128]{1,0:T(8,128)(2,1)} %get-tuple-element.14.refs_2_, ...), custom_call_target="tpu_custom_call" | custom-call | tf_op jit(solution)/shard_map/pallas_call | solution.py:413
